TPU v7x, 32 devices: a whole 2x2x4 slice. The times are simulated.
32 devices in a mesh: seq: 16 (over z, x, core), chan: 2 (over y).
Axes of the slice: x: 2, y: 2, z: 4, core: 2. Of those that a mesh axis runs over, the one named last changes fastest.
Arguments:
- inputs: bfloat16 [512, 262144], P('chan', 'seq'), may hold values from -6 to 6
- gate_acts: bfloat16 [512, 262144], P('chan', 'seq'), may hold values from -6 to 6
- out_grad: bfloat16 [512, 262144], P('chan', 'seq'), may hold values from -6 to 6
- first_factor: bfloat16 [512, 512], replicated, may hold values from -0.25 to 0.25
- second_factor: bfloat16 [512, 512], replicated, may hold values from -0.25 to 0.25
Outputs:
- input_grad: bfloat16 [512, 262144], P('chan', 'seq')
- gate_grad: bfloat16 [512, 262144], P('chan', 'seq')
- first_grad: float32 [512, 512], P('seq')
- second_grad: float32 [512, 512], P('seq')
All inputs are finite; a program needn't handle non-finite values.
Results may differ from a plain program's by a relative error of at most 0.0057.
Values may be sent and summed in bfloat16 or wider, within the bound.
A program may use at most 192 MiB of HBM per device.

v0:
```python
import jax
import jax.numpy as jnp
from jax import lax
from jax.sharding import PartitionSpec as P


def reduce_factors(first_term, second_term):
    totals = lax.psum((first_term, second_term), "chan")
    return (
        lax.psum_scatter(totals[0], "seq", scatter_dimension=0, tiled=True),
        lax.psum_scatter(totals[1], "seq", scatter_dimension=0, tiled=True),
    )


def local(inputs, gate_acts, out_grad, first_factor, second_factor):
    sequence_count = lax.axis_size("seq")
    chan_width, local_extent = inputs.shape
    cols_total = first_factor.shape[0]
    rows_total = second_factor.shape[0]
    row_block = rows_total // sequence_count
    col_block = cols_total // sequence_count
    grid_rows = inputs.reshape(chan_width, row_block, cols_total)
    first_blocks = first_factor.reshape(sequence_count, col_block, cols_total)
    second_block_list = second_factor.reshape(rows_total, sequence_count, row_block)
    outgoing_grid = jnp.einsum(
        "cij,skj->skic", grid_rows, first_blocks, preferred_element_type=jnp.float32
    ).astype(jnp.bfloat16)
    received_grid = lax.all_to_all(
        outgoing_grid.reshape(sequence_count, -1), "seq", split_axis=0, concat_axis=0, tiled=True
    )
    received_grid = received_grid.reshape(sequence_count, col_block, row_block, chan_width)
    mixed_out = jnp.einsum(
        "odgi,fog->idf", received_grid, second_block_list, preferred_element_type=jnp.float32
    )
    gate_vals = gate_acts.reshape(chan_width, col_block, rows_total).astype(jnp.float32)
    gradient_entries = out_grad.reshape(chan_width, col_block, rows_total).astype(jnp.float32)
    gate_grad = (
        (gradient_entries * mixed_out).astype(jnp.bfloat16).reshape(chan_width, local_extent)
    )
    mixer_gradient = (gradient_entries * gate_vals).astype(jnp.bfloat16)
    back_grid = jnp.einsum(
        "vph,hox->opxv", mixer_gradient, second_block_list, preferred_element_type=jnp.float32
    ).astype(jnp.bfloat16)
    second_term = jnp.einsum(
        "wjq,ajtw->qat", mixer_gradient, received_grid, preferred_element_type=jnp.float32
    ).reshape(rows_total, rows_total)
    returned = lax.all_to_all(
        back_grid.reshape(sequence_count, -1), "seq", split_axis=0, concat_axis=0, tiled=True
    )
    returned = returned.reshape(sequence_count, col_block, row_block, chan_width)
    input_grad = jnp.einsum(
        "skrc,skj->crj", returned, first_blocks, preferred_element_type=jnp.float32
    )
    input_grad = input_grad.astype(jnp.bfloat16).reshape(chan_width, local_extent)
    first_term = jnp.einsum(
        "skrc,crj->skj", returned, grid_rows, preferred_element_type=jnp.float32
    ).reshape(cols_total, cols_total)
    first_grad, second_grad = reduce_factors(first_term, second_term)
    return (input_grad, gate_grad, first_grad, second_grad)


def solution(mesh):
    return jax.shard_map(
        local,
        mesh=mesh,
        in_specs=(P("chan", "seq"), P("chan", "seq"), P("chan", "seq"), P(), P()),
        out_specs=(P("chan", "seq"), P("chan", "seq"), P("seq", None), P("seq", None)),
        check_vma=False,
    )
```

profile of v0, /device:TPU:0, one launch (start us, length us, event | category | flops | bytes accessed | tf_op | source)
XLA Modules:
  0.0 769.2 jit_solution(2571376017346037333)
XLA Ops:
  8.5 11.9 %copy.33 = bf16[256,16384]{0,1:T(8,128)(2,1)} copy(bf16[256,16384]{1,0:T(8,128)(2,1)} %param.6) | data formatting | bytes 16777216 | tf_op args[1]
  54.2 14.4 %all_to_all.16 = bf16[16,1,262144]{2,1,0:T(2,128)(2,1)} reshape(bf16[16,32,32,256]{3,2,1,0:T(8,128)(2,1)} %copy.36) | data formatting | bytes 16777216 | tf_op jit(solution)/shard_map/all_to_all | solution.py:47
  69.1 51.9 %reduce.2 = bf16[16,262144]{1,0:T(8,128)(2,1)} reduce(bf16[16,1,262144]{2,1,0:T(2,128)(2,1)} %all_to_all.16, bf16[]{:T(256)} %broadcast.2), dimensions={1}, to_apply=%all_to_all.16.reduce_sub_computation | reduce | bytes 16777218 | tf_op jit(solution)/shard_map/all_to_all | solution.py:47
  121.0 12.1 %reshape.69 = bf16[16,2,131072]{2,1,0:T(2,128)(2,1)} reshape(bf16[16,262144]{1,0:T(8,128)(2,1)} %reduce.2) | data formatting | bytes 16777216
  150.8 12.3 %copy.41 = bf16[16,32,32,256]{3,2,1,0:T(8,128)(2,1)} copy(bf16[16,32,32,256]{3,1,2,0:T(8,128)(2,1)} %convert_bitcast_fusion) | data formatting | bytes 16777216 | tf_op jit(solution)/shard_map/convert_element_type | solution.py:27
  163.1 14.4 %all_to_all.17 = bf16[16,1,262144]{2,1,0:T(2,128)(2,1)} reshape(bf16[16,32,32,256]{3,2,1,0:T(8,128)(2,1)} %copy.41) | data formatting | bytes 16777216 | tf_op jit(solution)/shard_map/all_to_all | solution.py:28
  177.5 51.8 %reduce.3 = bf16[16,262144]{1,0:T(8,128)(2,1)} reduce(bf16[16,1,262144]{2,1,0:T(2,128)(2,1)} %all_to_all.17, bf16[]{:T(256)} %broadcast.2), dimensions={1}, to_apply=%all_to_all.17.reduce_sub_computation | reduce | bytes 16777218 | tf_op jit(solution)/shard_map/all_to_all | solution.py:28
  229.3 12.4 %reshape.71 = bf16[16,2,131072]{2,1,0:T(2,128)(2,1)} reshape(bf16[16,262144]{1,0:T(8,128)(2,1)} %reduce.3) | data formatting | bytes 16777216
  241.7 49.5 %all-to-all-done = bf16[16,2,131072]{2,1,0:T(2,128)(2,1)} async-done(((bf16[16,2,131072]{2,1,0:T(2,128)(2,1)}), bf16[16,2,131072]{2,1,0:T(2,128)(2,1)}, u32[]{:S(2)}, u32[]{:S(2)}) %all-to-all-start) | async-done | bytes 8388640 | tf_op jit(solution)/shard_map/all_to_all | solution.py:47
  291.2 36.5 %all-to-all-start.1 = ((bf16[16,2,131072]{2,1,0:T(2,128)(2,1)}), bf16[16,2,131072]{2,1,0:T(2,128)(2,1)}, u32[]{:S(2)}, u32[]{:S(2)}) async-start(bf16[16,2,131072]{2,1,0:T(2,128)(2,1)} %reshape.71), calls=%async_computation.1 | async-start | bytes 16777216 | tf_op jit(solution)/shard_map/all_to_all | solution.py:28
  327.8 16.4 %reshape.70 = bf16[16,1,262144]{2,1,0:T(2,128)(2,1)} reshape(bf16[16,2,131072]{2,1,0:T(2,128)(2,1)} %all-to-all-done) | data formatting | bytes 16777216
  344.2 51.4 %reduce = bf16[16,262144]{1,0:T(8,128)(2,1)} reduce(bf16[16,1,262144]{2,1,0:T(2,128)(2,1)} %reshape.70, bf16[]{:T(256)} %constant), dimensions={1}, to_apply=%all_to_all.13.reduce_sub_computation | reduce | bytes 16777218 | tf_op jit(solution)/shard_map/all_to_all | solution.py:47
  426.7 12.8 %copy.43 = f32[256,32,512]{2,0,1:T(8,128)} copy(bf16[256,32,512]{0,2,1:T(8,128)(2,1)} %bitcast.83) | data formatting | bytes 25165824 | tf_op jit(solution)/shard_map/convert_element_type | solution.py:36
  439.5 43.3 %all-to-all-done.1 = bf16[16,2,131072]{2,1,0:T(2,128)(2,1)} async-done(((bf16[16,2,131072]{2,1,0:T(2,128)(2,1)}), bf16[16,2,131072]{2,1,0:T(2,128)(2,1)}, u32[]{:S(2)}, u32[]{:S(2)}) %all-to-all-start.1) | async-done | bytes 8388640 | tf_op jit(solution)/shard_map/all_to_all | solution.py:28
  482.8 16.4 %reshape.72 = bf16[16,1,262144]{2,1,0:T(2,128)(2,1)} reshape(bf16[16,2,131072]{2,1,0:T(2,128)(2,1)} %all-to-all-done.1) | data formatting | bytes 16777216
  499.2 51.2 %reduce.1 = bf16[16,262144]{1,0:T(8,128)(2,1)} reduce(bf16[16,1,262144]{2,1,0:T(2,128)(2,1)} %reshape.72, bf16[]{:T(256)} %constant), dimensions={1}, to_apply=%all_to_all.15.reduce_sub_computation | reduce | bytes 16777218 | tf_op jit(solution)/shard_map/all_to_all | solution.py:28
  566.9 13.7 %fusion.14 = f32[512,512]{1,0:T(8,128)} fusion(bf16[512,32,256]{2,0,1:T(8,128)(2,1)} %bitcast.95, bf16[256,32,512]{0,2,1:T(8,128)(2,1)} %bitcast.85, bf16[256,32,512]{0,2,1:T(8,128)(2,1)} %bitcast.84), kind=kOutput, calls=%fused_computation.17 | convolution fusion | flops 4311744512 | bytes 26214400 | tf_op jit(solution)/shard_map/wjq,ajtw->qat/dot_general | solution.py:44
  580.6 12.7 %fusion = bf16[256,32,512]{2,0,1:T(8,128)(2,1)} fusion(f32[256,32,512]{2,0,1:T(8,128)} %copy.43, bf16[16,32,32,256]{3,2,1,0:T(8,128)(2,1)} %bitcast.89, bf16[512,16,32,1]{0,2,3,1:T(8,128)(2,1)S(1)} %bitcast.98), kind=kOutput, calls=%fused_computation.1 | convolution fusion | flops 4303355904 | bytes 34078720 | tf_op jit(solution)/shard_map/odgi,fog->idf/dot_general | solution.py:32
  593.3 78.7 %reduce-scatter.5.cloned.1.call-done = f32[32,512]{1,0:T(8,128)} async-done(((f32[512,512]{1,0:T(8,128)}), f32[32,512]{1,0:T(8,128)}) %reduce-scatter.5.cloned.1.call-update) | async-done | bytes 65552 | tf_op jit(solution)/shard_map/reduce_scatter | solution.py:11
  672.0 39.8 %fusion.8 = bf16[256,32,512]{2,0,1:T(8,128)(2,1)} fusion(bf16[16,32,512,1]{2,1,0,3:T(8,128)(2,1)S(1)} %bitcast.81, bf16[16,32,32,256]{3,2,1,0:T(8,128)(2,1)} %bitcast.87), kind=kOutput, calls=%fused_computation.15 | convolution fusion | flops 4299161600 | bytes 17301504 | tf_op jit(solution)/shard_map/skrc,skj->crj/dot_general | solution.py:51
  711.8 11.9 %copy.39 = bf16[256,32,512]{0,2,1:T(8,128)(2,1)} copy(bf16[256,32,512]{2,0,1:T(8,128)(2,1)} %fusion.8) | data formatting | bytes 16777216 | tf_op jit(solution)/shard_map/convert_element_type | solution.py:54
  723.8 11.9 %copy.48 = bf16[256,16384]{1,0:T(8,128)(2,1)} copy(bf16[256,16384]{0,1:T(8,128)(2,1)} %bitcast.92) | data formatting | bytes 16777216
  735.7 11.9 %copy.44 = bf16[256,32,512]{0,2,1:T(8,128)(2,1)} copy(bf16[256,32,512]{2,0,1:T(8,128)(2,1)} %fusion) | data formatting | bytes 16777216 | tf_op jit(solution)/shard_map/convert_element_type | solution.py:38
  747.6 11.9 %copy.49 = bf16[256,16384]{1,0:T(8,128)(2,1)} copy(bf16[256,16384]{0,1:T(8,128)(2,1)} %bitcast.93) | data formatting | bytes 16777216
  (25 shorter events, 104.0 us)
Async XLA Ops:
  7.2 133.4 %copy-start = (bf16[512,512]{1,0:T(8,128)(2,1)S(1)}, bf16[512,512]{1,0:T(8,128)(2,1)}, u32[]{:S(2)}) copy-start(bf16[512,512]{1,0:T(8,128)(2,1)} %param.8) | copy-start | bytes 1572868
  133.1 158.1 %all-to-all-start = ((bf16[16,2,131072]{2,1,0:T(2,128)(2,1)}), bf16[16,2,131072]{2,1,0:T(2,128)(2,1)}, u32[]{:S(2)}, u32[]{:S(2)}) async-start(bf16[16,2,131072]{2,1,0:T(2,128)(2,1)} %reshape.69), calls=%async_computation | async-start | bytes 16777216 | tf_op jit(solution)/shard_map/all_to_all | solution.py:47
  291.2 191.6 %all-to-all-start.1 = ((bf16[16,2,131072]{2,1,0:T(2,128)(2,1)}), bf16[16,2,131072]{2,1,0:T(2,128)(2,1)}, u32[]{:S(2)}, u32[]{:S(2)}) async-start(bf16[16,2,131072]{2,1,0:T(2,128)(2,1)} %reshape.71), calls=%async_computation.1 | async-start | bytes 16777216 | tf_op jit(solution)/shard_map/all_to_all | solution.py:28
  327.8 265.5 %reduce-scatter.3.cloned.1.call-start = ((), (), s32[]{:S(2)}) async-start(), calls=%async_computation.4 | async-start | bytes 1114112 | tf_op jit(solution)/shard_map/reduce_scatter | solution.py:10
  426.7 245.3 %reduce-scatter.5.cloned.1.call-start = ((), (), s32[]{:S(2)}) async-start(), calls=%async_computation.5 | async-start | bytes 1114112 | tf_op jit(solution)/shard_map/reduce_scatter | solution.py:11
  580.5 179.0 %all-reduce.3.cloned.1.call-start = ((), (), s32[]{:S(2)}) async-start(), calls=%async_computation.6 | async-start | bytes 262144 | tf_op jit(solution)/shard_map/psum | solution.py:8
Sparse Core Ops, SparseCore 0:
  426.8 86.7 reduce-scatter.2
  580.7 91.2 reduce-scatter.4
  674.3 20.5 all-reduce.2
where the time goes:
time: 780 us; the launch traced here: 769 us
  local copies, waits for them, and re-layouts  232 us (30%)
  other arithmetic  213 us (27%)
  waiting for transfers between devices  172 us (22%)
  matrix products  94.6 us (12%)
  starting transfers between devices  44.1 us (6%)
  between operations  14 us (2%)
    unnamed x15, local copies, waits for them, and re-layouts  126 us
    all_to_all x2, other arithmetic, local(): lax.all_to_all(back_grid.reshape(sequence_count, -1), 'seq', split_axis=0...  103 us
    all_to_all x2, other arithmetic, local(): lax.all_to_all(outgoing_grid.reshape(sequence_count, -1), 'seq', split_ax...  103 us
    reduce_scatter x1, waiting for transfers between devices, reduce_factors(): lax.psum_scatter(totals[1], 'seq', scatter_dimension=0, tiled=True)  78.7 us
    all_to_all x1, waiting for transfers between devices, local(): lax.all_to_all(back_grid.reshape(sequence_count, -1), 'seq', split_axis=0...  49.5 us
    all_to_all x1, waiting for transfers between devices, local(): lax.all_to_all(outgoing_grid.reshape(sequence_count, -1), 'seq', split_ax...  43.3 us
    dot_general x1, matrix products, local(): jnp.einsum('skrc,skj->crj', returned, first_blocks, preferred_element_typ...  39.8 us
    all_to_all x1, starting transfers between devices, local(): lax.all_to_all(outgoing_grid.reshape(sequence_count, -1), 'seq', split_ax...  36.5 us
  transfers between devices with their start and end apart: 5, of which 3 were waited for; matrix products, arithmetic and copies ran while one was open for 52% of the time, Pallas kernels for 0%

commit v1 on v0

v1 whole, which is shorter than its diff:
```python
import functools

import jax
import jax.numpy as jnp
from jax import lax
from jax.experimental import pallas as pl
from jax.experimental.pallas import tpu as pltpu
from jax.sharding import PartitionSpec as P

BF16 = jnp.bfloat16
F32 = jnp.float32
LANES = 128
PACK = 16
GROUPS = 4


def dot_nn(lhs, rhs):
    return lax.dot_general(lhs, rhs, (((1,), (0,)), ((), ())), preferred_element_type=F32)


def dot_nt(lhs, rhs):
    return lax.dot_general(lhs, rhs, (((1,), (1,)), ((), ())), preferred_element_type=F32)


def dot_tn(lhs, rhs):
    return lax.dot_general(lhs, rhs, (((0,), (0,)), ((), ())), preferred_element_type=F32)


def stream(count, loads, work, store=None):
    def body(step, carry):
        slot = lax.rem(step, 2)

        @pl.when(step + 1 < count)
        def _():
            for load in loads:
                load(step + 1, 1 - slot).start()

        for load in loads:
            load(step, slot).wait()
        if store is not None:

            @pl.when(step >= 2)
            def _():
                store(step - 2, slot).wait()

        work(step, slot)
        if store is not None:
            store(step, slot).start()
        return carry

    for load in loads:
        load(0, 0).start()
    lax.fori_loop(0, count, body, 0)
    if store is not None:
        for step in range(max(count - 2, 0), count):
            store(step, step % 2).wait()


def kernel(
    n, x_hbm, q_hbm, g_hbm, a_ref, bt_ref,
    dx_hbm, dq_hbm, acc1, acc2,
    out1, out2, got1, got2, turned, x_buf, g_buf, q_buf, y_buf,
    x_sem, g_sem, q_sem, y_sem, own_sem, send1, recv1, send2, recv2,
):
    me = lax.axis_index("seq")
    width = x_hbm.shape[0]
    rows, cols = bt_ref.shape[0], a_ref.shape[0]
    row_block, col_block = rows // n, cols // n
    part = row_block // GROUPS

    def hop(d):
        return lax.rem(me + d, n)

    barrier = pltpu.get_barrier_semaphore()

    def greet(d, carry):
        pl.semaphore_signal(
            barrier, inc=1, device_id={"seq": hop(d)}, device_id_type=pl.DeviceIdType.MESH
        )
        return carry

    lax.fori_loop(1, n, greet, 0)

    def load_x(step, slot):
        return pltpu.make_async_copy(
            x_hbm.at[:, pl.ds(pl.multiple_of(step * cols, LANES), cols)],
            x_buf.at[slot], x_sem.at[slot],
        )

    def load_g(step, slot):
        return pltpu.make_async_copy(
            g_hbm.at[:, pl.ds(pl.multiple_of(step * rows, LANES), rows)],
            g_buf.at[slot], g_sem.at[slot],
        )

    def load_q(step, slot):
        return pltpu.make_async_copy(
            q_hbm.at[:, pl.ds(pl.multiple_of(step * rows, LANES), rows)],
            q_buf.at[slot], q_sem.at[slot],
        )

    def send_first(group, peer):
        return pltpu.make_async_remote_copy(
            src_ref=out1.at[
                pl.ds(group * part, part), pl.ds(pl.multiple_of(peer * col_block, PACK), col_block)
            ],
            dst_ref=got1.at[pl.ds(me * row_block + group * part, part)],
            send_sem=send1.at[group], recv_sem=recv1.at[group],
            device_id={"seq": peer}, device_id_type=pl.DeviceIdType.MESH,
        )

    def first_own():
        return pltpu.make_async_copy(
            out1.at[:, pl.ds(pl.multiple_of(me * col_block, PACK), col_block)],
            got1.at[pl.ds(me * row_block, row_block)], own_sem.at[0],
        )

    def chunk_view(ref, start, count, h, ch):
        return ref.at[
            pl.ds(start, count), pl.ds(h * PACK, PACK), pl.ds(ch * LANES, LANES)
        ]

    lane_parts = width // LANES
    chunks = [(h, ch) for h in range(row_block // PACK) for ch in range(lane_parts)]

    def send_second(index, peer):
        h, ch = chunks[index]
        return pltpu.make_async_remote_copy(
            src_ref=out2.at[
                :, pl.ds(pl.multiple_of(peer * row_block + h * PACK, PACK), PACK),
                pl.ds(ch * LANES, LANES),
            ],
            dst_ref=chunk_view(got2, me * col_block, col_block, h, ch),
            send_sem=send2.at[index], recv_sem=recv2.at[index],
            device_id={"seq": peer}, device_id_type=pl.DeviceIdType.MESH,
        )

    def second_own():
        return pltpu.make_async_copy(
            out2.at[:, pl.ds(pl.multiple_of(me * row_block, PACK), row_block)],
            got2.at[pl.ds(me * col_block, col_block)], own_sem.at[1],
        )

    def to_all(send, index):
        def body(d, carry):
            send(index, hop(d)).start()
            return carry

        lax.fori_loop(1, n, body, 0)

    def await_first(sem):
        view = got1.at[pl.ds(0, (n - 1) * part)]
        pltpu.make_async_copy(view, view, sem).wait()

    def await_second(index, sem):
        h, ch = chunks[index]
        view = chunk_view(got2, 0, (n - 1) * col_block, h, ch)
        pltpu.make_async_copy(view, view, sem).wait()

    for group in range(GROUPS):
        def inner_step(step, slot):
            out1[group * part + step] = dot_nt(a_ref[...], x_buf[slot]).astype(BF16)

        stream(part, [lambda s, slot, group=group: load_x(group * part + s, slot)], inner_step)
        if group == 0:
            pl.semaphore_wait(barrier, n - 1)
        to_all(send_first, group)
    first_own().start()

    def back_step(step, slot):
        mg = (g_buf[slot].astype(F32) * q_buf[slot].astype(F32)).astype(BF16)
        out2[step] = dot_nt(bt_ref[...], mg).astype(BF16)

    stream(col_block, [load_g, load_q], back_step)
    second_own().start()

    acc1[...] = jnp.zeros_like(acc1)
    acc2[...] = jnp.zeros_like(acc2)

    for group in range(GROUPS - 1):
        await_first(recv1.at[group])
    early = max(len(chunks) // 2, 1)
    for index in range(early):
        to_all(send_second, index)
    await_first(recv1.at[GROUPS - 1])
    first_own().wait()

    def turn(got, h, ch, slot, total):
        def body(block, carry):
            start = pl.multiple_of(block * 8, 8)
            value = got[pl.ds(start, 8), pl.ds(h * PACK, PACK), pl.ds(ch * LANES, LANES)]
            turned[slot, pl.ds(pl.multiple_of(block * 8 * PACK, 8 * PACK), 8 * PACK), :] = (
                value.astype(F32).reshape(8 * PACK, LANES)
            )
            return carry

        lax.fori_loop(0, total // 8, body, 0)

    def pick(slot, step, total):
        return turned[slot, pl.ds(step, total, stride=PACK), :].astype(BF16)

    later = list(range(early, len(chunks)))
    halves = col_block // PACK
    for h in range(halves):
        for ch in range(lane_parts):
            turn(got1, h, ch, ch, rows)

        def gate_step(step, slot):
            g = g_buf[slot].astype(F32)
            mg = (g * q_buf[slot].astype(F32)).astype(BF16)
            inner = jnp.concatenate([pick(ch, step, rows) for ch in range(lane_parts)], axis=1)
            y_buf[slot] = (g * dot_tn(inner, bt_ref[...])).astype(BF16)
            acc2[...] += dot_nn(inner, mg)

        def store_dq(step, slot):
            return pltpu.make_async_copy(
                y_buf.at[slot],
                dq_hbm.at[:, pl.ds(pl.multiple_of((h * PACK + step) * rows, LANES), rows)],
                y_sem.at[slot],
            )

        stream(
            PACK,
            [lambda s, slot: load_g(h * PACK + s, slot), lambda s, slot: load_q(h * PACK + s, slot)],
            gate_step, store_dq,
        )
        share = later if h == halves - 1 else later[: max(len(later) // 2, 0)]
        for index in share:
            to_all(send_second, index)
        later = [index for index in later if index not in share]

    second_own().wait()
    for index, (h, ch) in enumerate(chunks):
        await_second(index, recv2.at[index])
        turn(got2, h, ch, 0, cols)
        span = pl.ds(ch * LANES, LANES)

        def block(ref, step):
            start = pl.multiple_of((h * PACK + step) * cols, LANES)
            return ref.at[span, pl.ds(start, cols)]

        def load_part(step, slot):
            return pltpu.make_async_copy(
                block(x_hbm, step), x_buf.at[slot, pl.ds(0, LANES)], x_sem.at[slot]
            )

        def store_part(step, slot):
            return pltpu.make_async_copy(
                y_buf.at[slot, pl.ds(0, LANES)], block(dx_hbm, step), y_sem.at[slot]
            )

        def input_step(step, slot):
            inner_grad = pick(0, step, cols)
            y_buf[slot, pl.ds(0, LANES)] = dot_tn(inner_grad, a_ref[...]).astype(BF16)
            acc1[...] += dot_nn(inner_grad, x_buf[slot, pl.ds(0, LANES)])

        stream(PACK, [load_part], input_step, store_part)

    for group in range(GROUPS):
        await_first(send1.at[group])
    for index in range(len(chunks)):
        await_second(index, send2.at[index])


def fused(inputs, gate_acts, out_grad, first_factor, second_factor):
    n = lax.axis_size("seq")
    width, extent = inputs.shape
    cols, rows = first_factor.shape[0], second_factor.shape[0]
    row_block, col_block = rows // n, cols // n
    chunk_count = (row_block // PACK) * (width // LANES)
    vmem = pl.BlockSpec(memory_space=pltpu.VMEM)
    hbm = pl.BlockSpec(memory_space=pl.ANY)
    dma = pltpu.SemaphoreType.DMA
    long_side = max(rows, cols)
    flops = 12 * width * row_block * cols * rows
    return pl.pallas_call(
        functools.partial(kernel, n),
        out_shape=(
            jax.ShapeDtypeStruct((width, extent), BF16),
            jax.ShapeDtypeStruct((width, extent), BF16),
            jax.ShapeDtypeStruct((cols, cols), F32),
            jax.ShapeDtypeStruct((rows, rows), F32),
        ),
        in_specs=[hbm, hbm, hbm, vmem, vmem],
        out_specs=(hbm, hbm, vmem, vmem),
        scratch_shapes=[
            pltpu.VMEM((row_block, cols, width), BF16),
            pltpu.VMEM((col_block, rows, width), BF16),
            pltpu.VMEM((rows, col_block, width), BF16),
            pltpu.VMEM((cols, row_block, width), BF16),
            pltpu.VMEM((width // LANES, long_side * PACK, LANES), F32),
            pltpu.VMEM((2, width, cols), BF16),
            pltpu.VMEM((2, width, rows), BF16),
            pltpu.VMEM((2, width, rows), BF16),
            pltpu.VMEM((2, width, long_side), BF16),
            dma((2,)), dma((2,)), dma((2,)), dma((2,)), dma((2,)),
            dma((GROUPS,)), dma((GROUPS,)), dma((chunk_count,)), dma((chunk_count,)),
        ],
        compiler_params=pltpu.CompilerParams(
            collective_id=0, has_side_effects=True, vmem_limit_bytes=56 * 2**20
        ),
        cost_estimate=pl.CostEstimate(flops=flops, bytes_accessed=16 * width * extent, transcendentals=0),
    )(inputs, gate_acts, out_grad, first_factor, second_factor.T)


def plain(inputs, gate_acts, out_grad, first_factor, second_factor):
    n = lax.axis_size("seq")
    width, extent = inputs.shape
    cols, rows = first_factor.shape[0], second_factor.shape[0]
    row_block, col_block = rows // n, cols // n
    grid = inputs.reshape(width, row_block, cols)
    first = first_factor.reshape(n, col_block, cols)
    second = second_factor.reshape(rows, n, row_block)

    def exchange(value):
        sent = lax.all_to_all(
            value.reshape(n, -1), "seq", split_axis=0, concat_axis=0, tiled=True
        )
        return sent.reshape(n, col_block, row_block, width)

    def einsum(spec, lhs, rhs):
        return jnp.einsum(spec, lhs, rhs, preferred_element_type=F32)

    received = exchange(einsum("cij,skj->skic", grid, first).astype(BF16))
    mixed = einsum("odgi,fog->idf", received, second)
    g = out_grad.reshape(width, col_block, rows).astype(F32)
    gate_grad = (g * mixed).astype(BF16).reshape(width, extent)
    mg = (g * gate_acts.reshape(width, col_block, rows).astype(F32)).astype(BF16)
    returned = exchange(einsum("vph,hox->opxv", mg, second).astype(BF16))
    second_term = einsum("wjq,ajtw->qat", mg, received).reshape(rows, rows)
    input_grad = einsum("skrc,skj->crj", returned, first).astype(BF16).reshape(width, extent)
    first_term = einsum("skrc,crj->skj", returned, grid).reshape(cols, cols)
    return input_grad, gate_grad, first_term, second_term


def local(inputs, gate_acts, out_grad, first_factor, second_factor):
    n = lax.axis_size("seq")
    width = inputs.shape[0]
    cols, rows = first_factor.shape[0], second_factor.shape[0]
    fits = width % LANES == 0 and rows % (n * PACK) == 0 and cols % (n * PACK) == 0
    args = (inputs, gate_acts, out_grad, first_factor, second_factor)
    if fits:
        input_grad, gate_grad, first_term, second_term = fused(*args)
        second_term = second_term.T
    else:
        input_grad, gate_grad, first_term, second_term = plain(*args)
    totals = lax.psum((first_term, second_term), "chan")
    first_grad = lax.psum_scatter(totals[0], "seq", scatter_dimension=0, tiled=True)
    second_grad = lax.psum_scatter(totals[1], "seq", scatter_dimension=0, tiled=True)
    return input_grad, gate_grad, first_grad, second_grad


def solution(mesh):
    return jax.shard_map(
        local,
        mesh=mesh,
        in_specs=(P("chan", "seq"), P("chan", "seq"), P("chan", "seq"), P(), P()),
        out_specs=(P("chan", "seq"), P("chan", "seq"), P("seq", None), P("seq", None)),
        check_vma=False,
    )
```

time: 780 us -> 570 us (0.73); the launches traced: 769 us -> 567 us
  Pallas kernels: 0 us -> 370 us
  other arithmetic: 213 us -> 0 us
  local copies, waits for them, and re-layouts: 232 us -> 23.9 us
  matrix products: 94.6 us -> 0 us
  starting transfers between devices: 44.1 us -> 0.12 us
  waiting for transfers between devices: 172 us -> 159 us
    pallas_call x0 -> x1, Pallas kernels: none -> 370 us  [fused(): pl.pallas_call(functools.partial(kernel, n), out_shape=(jax.ShapeDtypeStr...]
    all_to_all x4 -> x0, other arithmetic: 206 us -> none  [the longest x2 103 us: local(): lax.all_to_all(back_grid.reshape(sequence_count, -1), 'seq', split_axis=0...]
    unnamed x15 -> x9, local copies, waits for them, and re-layouts: 126 us -> 23.9 us
    dot_general x6 -> x0, matrix products: 94.6 us -> none  [the longest x1 39.8 us: local(): jnp.einsum('skrc,skj->crj', returned, first_blocks, preferred_element_typ...]
    all_to_all x2 -> x0, waiting for transfers between devices: 92.8 us -> none  [the longest x1 49.5 us: local(): lax.all_to_all(back_grid.reshape(sequence_count, -1), 'seq', split_axis=0...]
    unnamed x3 -> x4, waiting for transfers between devices: 0.05 us -> 74 us
    convert_element_type x5 -> x0, local copies, waits for them, and re-layouts: 57 us -> none  [the longest x1 12.8 us: local(): out_grad.reshape(chan_width, col_block, rows_total).astype(jnp.float32)]
    all_to_all x2 -> x0, starting transfers between devices: 44 us -> none  [the longest x1 36.5 us: local(): lax.all_to_all(outgoing_grid.reshape(sequence_count, -1), 'seq', split_ax...]
  transfers between devices with their start and end apart: 5 -> 3, of which waited for: 3 -> 3; matrix products, arithmetic and copies ran while one was open for 52% -> 0% of each run, Pallas kernels for 0% -> 0%
where the time goes in v1:
time: 570 us; the launch traced here: 567 us
  Pallas kernels  370 us (65%)
  waiting for transfers between devices  159 us (28%)
  local copies, waits for them, and re-layouts  23.9 us (4%)
  between operations  13.8 us (2%)
    pallas_call x1, Pallas kernels, fused(): pl.pallas_call(functools.partial(kernel, n), out_shape=(jax.ShapeDtypeStr...  370 us
    unnamed x4, waiting for transfers between devices  74 us
    reduce_scatter x1, waiting for transfers between devices, local(): lax.psum_scatter(totals[0], 'seq', scatter_dimension=0, tiled=True)  58.8 us
    psum x1, waiting for transfers between devices, local(): totals = lax.psum((first_term, second_term), 'chan')  26.4 us
    unnamed x9, local copies, waits for them, and re-layouts  23.9 us
  transfers between devices with their start and end apart: 3, of which 3 were waited for; matrix products, arithmetic and copies ran while one was open for 0% of the time, Pallas kernels for 0%

profile of v1, /device:TPU:0, one launch (start us, length us, event | category | flops | bytes accessed | tf_op | source)
XLA Modules:
  0.0 567.4 jit_solution(12730573571328018456)
XLA Ops:
  7.2 0.0 reduce-scatter.7.cloned.1.call-start
  7.2 2.0 copy.11
  9.3 370.5 %shard_map.84 = (bf16[256,16384]{1,0:T(8,128)(2,1)}, bf16[256,16384]{1,0:T(8,128)(2,1)}, f32[512,512]{1,0:T(8,128)}, f32[512,512]{1,0:T(8,128)}) custom-call(bf16[256,16384]{1,0:T(8,128)(2,1)} %x_hbm.1, bf16[256,16384]{1,0:T(8,128)(2,1)} %q_hbm.1, bf16[256,16384]{1,0:T(8,128)(2,1)} %g_hbm.1, bf16[512,512]{1,0:T(8,128)(2,1)} %a_ref.1, bf16[512,512]{1,0:T(8,128)(2,1)} %bitcast.4), custom_call_target="tpu_custom_call" | custom-call | flops 25769803776 | bytes 67108864 | tf_op jit(solution)/shard_map/pallas_call | solution.py:276
  379.7 2.5 copy.13
  382.3 0.0 reduce-scatter.7.cloned.1.call-update
  382.3 0.0 reduce-scatter.5.cloned.1.call-start
  382.3 0.7 reduce-scatter.5.cloned.1.call-update
  383.0 0.0 all-reduce.3.cloned.1.call-start
  383.1 73.2 %reduce-scatter.7.cloned.1.call-done = f32[32,512]{1,0:T(8,128)} async-done(((f32[512,512]{1,0:T(8,128)}), f32[32,512]{1,0:T(8,128)}) %reduce-scatter.7.cloned.1.call-update) | async-done | bytes 65552
  456.3 1.7 copy.14
  458.0 58.8 %reduce-scatter.5.cloned.1.call-done = f32[32,512]{1,0:T(8,128)} async-done(((f32[512,512]{1,0:T(8,128)}), f32[32,512]{1,0:T(8,128)}) %reduce-scatter.5.cloned.1.call-update) | async-done | bytes 65552 | tf_op jit(solution)/shard_map/reduce_scatter | solution.py:348
  516.8 0.0 all-reduce.3.cloned.1.call-update
  516.8 26.4 %all-reduce.3.cloned.1.call-done = (f32[32,512]{1,0:T(8,128)}, f32[32,512]{0,1:T(8,128)}) async-done(((f32[32,512]{1,0:T(8,128)}, f32[32,512]{0,1:T(8,128)}), (f32[32,512]{1,0:T(8,128)}, f32[32,512]{0,1:T(8,128)})) %all-reduce.3.cloned.1.call-update) | async-done | bytes 131088 | tf_op jit(solution)/shard_map/psum | solution.py:347
  543.2 1.7 copy.12
  544.9 7.7 %copy.19 = bf16[256,16384]{1,0:T(8,128)(2,1)} copy(bf16[256,16384]{1,0:T(8,128)(2,1)} %get-tuple-element.26) | data formatting | bytes 16777216
  552.5 0.0 copy-start
  552.5 7.7 %copy.20 = bf16[256,16384]{1,0:T(8,128)(2,1)} copy(bf16[256,16384]{1,0:T(8,128)(2,1)} %get-tuple-element.27) | data formatting | bytes 16777216
  560.2 0.0 copy-done
  560.2 0.6 copy.21
Async XLA Ops:
  7.2 449.2 %reduce-scatter.7.cloned.1.call-start = ((), (), s32[]{:S(2)}) async-start(), calls=%async_computation.3 | async-start | bytes 1114112
  382.3 134.5 %reduce-scatter.5.cloned.1.call-start = ((), (), s32[]{:S(2)}) async-start(), calls=%async_computation.2 | async-start | bytes 1114112 | tf_op jit(solution)/shard_map/reduce_scatter | solution.py:348
  383.0 160.1 %all-reduce.3.cloned.1.call-start = ((), (), s32[]{:S(2)}) async-start(), calls=%async_computation.4 | async-start | bytes 655360 | tf_op jit(solution)/shard_map/psum | solution.py:347
  552.5 7.7 %copy-start = (f32[32,512]{1,0:T(8,128)S(1)}, f32[32,512]{1,0:T(8,128)}, u32[]{:S(2)}) copy-start(f32[32,512]{1,0:T(8,128)} %get-tuple-element.28) | copy-start | bytes 196612
Sparse Core Ops, SparseCore 0:
  382.4 73.8 reduce-scatter.6
  460.4 56.3 reduce-scatter.4
  519.7 23.4 all-reduce.2

commit v2 on v1

--- a/solution.py
+++ b/solution.py
@@ -11,7 +11,7 @@
 F32 = jnp.float32
 LANES = 128
 PACK = 16
-GROUPS = 4
+GROUPS = 8
 
 
 def dot_nn(lhs, rhs):
@@ -57,19 +57,97 @@
 
 
 def kernel(
-    n, x_hbm, q_hbm, g_hbm, a_ref, bt_ref,
-    dx_hbm, dq_hbm, acc1, acc2,
-    out1, out2, got1, got2, turned, x_buf, g_buf, q_buf, y_buf,
-    x_sem, g_sem, q_sem, y_sem, own_sem, send1, recv1, send2, recv2,
+    n, chans, low, x_hbm, q_hbm, g_hbm, a_ref, b_ref,
+    dx_hbm, dq_hbm, d1_ref, d2_ref,
+    out1, out2, got1, got2, turned, x_buf, g_buf, q_buf, y_buf, bt_ref, acc1, acc2,
+    terms, land1, sums, land2, final,
+    x_sem, g_sem, q_sem, y_sem, own_sem, send1, recv1, send2, recv2, send_sum, recv_sum,
 ):
-    me = lax.axis_index("seq")
+    me, my_chan = lax.axis_index("seq"), lax.axis_index("chan")
     width = x_hbm.shape[0]
-    rows, cols = bt_ref.shape[0], a_ref.shape[0]
+    rows, cols = b_ref.shape[0], a_ref.shape[0]
     row_block, col_block = rows // n, cols // n
     part = row_block // GROUPS
 
     def hop(d):
         return lax.rem(me + d, n)
+
+    near, high = low * chans, n // low
+    my_low, my_high = lax.rem(me, low), me // low
+    my_near = my_low * chans + my_chan
+
+    def near_device(d):
+        slot = lax.rem(my_near + d, near)
+        return slot, {"seq": my_high * low + slot // chans, "chan": lax.rem(slot, chans)}
+
+    def remote(src, dst, kind, which, device):
+        return pltpu.make_async_remote_copy(
+            src_ref=src, dst_ref=dst,
+            send_sem=send_sum.at[kind, which], recv_sem=recv_sum.at[kind, which],
+            device_id=device, device_id_type=pl.DeviceIdType.MESH,
+        )
+
+    def await_sum(view, kind, which):
+        pltpu.make_async_copy(view, view, recv_sum.at[kind, which]).wait()
+        pltpu.make_async_copy(view, view, send_sum.at[kind, which]).wait()
+
+    def sum_near_start(which):
+        def body(d, carry):
+            slot, device = near_device(d)
+            remote(
+                terms.at[which, slot], land1.at[which, my_near], 0, which, device
+            ).start()
+            return carry
+
+        lax.fori_loop(1, near, body, 0)
+
+    def sum_far_start(which):
+        await_sum(land1.at[which, pl.ds(0, near - 1)], 0, which)
+        sums[which] = terms[which, my_near]
+
+        def add(d, carry):
+            sums[which] += land1[which, lax.rem(my_near + d, near)]
+            return carry
+
+        lax.fori_loop(1, near, add, 0)
+
+        def body(d, carry):
+            to = lax.rem(my_high + d, high)
+            remote(
+                sums.at[which, to], land2.at[which, my_high], 1, which,
+                {"seq": to * low + my_low, "chan": my_chan},
+            ).start()
+            return carry
+
+        lax.fori_loop(1, high, body, 0)
+
+    def sum_share_start(which):
+        await_sum(land2.at[which, pl.ds(0, high - 1)], 1, which)
+        final[which, my_chan] = sums[which, my_high]
+
+        def add(d, carry):
+            final[which, my_chan] += land2[which, lax.rem(my_high + d, high)]
+            return carry
+
+        lax.fori_loop(1, high, add, 0)
+
+        def body(d, carry):
+            remote(
+                final.at[which, my_chan], final.at[which, my_chan], 2, which,
+                {"seq": me, "chan": lax.rem(my_chan + d, chans)},
+            ).start()
+            return carry
+
+        lax.fori_loop(1, chans, body, 0)
+
+    def sum_end(which, out):
+        await_sum(final.at[which, pl.ds(0, chans - 1)], 2, which)
+        out[...] = final[which].reshape(out.shape)
+
+    def put_terms(which, strip, value):
+        share = row_block // chans
+        for c in range(chans):
+            terms[which, (strip % low) * chans + c, strip // low] = value[c * share:(c + 1) * share]
 
     barrier = pltpu.get_barrier_semaphore()
 
@@ -80,6 +158,19 @@
         return carry
 
     lax.fori_loop(1, n, greet, 0)
+
+    def greet_chan(d, carry):
+        def body(spot, inner):
+            pl.semaphore_signal(
+                barrier, inc=1,
+                device_id={"seq": my_high * low + spot, "chan": lax.rem(my_chan + d, chans)},
+                device_id_type=pl.DeviceIdType.MESH,
+            )
+            return inner
+
+        return lax.fori_loop(0, low, body, carry)
+
+    lax.fori_loop(1, chans, greet_chan, 0)
 
     def load_x(step, slot):
         return pltpu.make_async_copy(
@@ -157,15 +248,26 @@
         view = chunk_view(got2, 0, (n - 1) * col_block, h, ch)
         pltpu.make_async_copy(view, view, sem).wait()
 
-    for group in range(GROUPS):
-        def inner_step(step, slot):
-            out1[group * part + step] = dot_nt(a_ref[...], x_buf[slot]).astype(BF16)
-
-        stream(part, [lambda s, slot, group=group: load_x(group * part + s, slot)], inner_step)
-        if group == 0:
-            pl.semaphore_wait(barrier, n - 1)
-        to_all(send_first, group)
+    def inner_step(first, step, slot):
+        out1[first + step] = dot_nt(a_ref[...], x_buf[slot]).astype(BF16)
+
+    stream(part, [load_x], functools.partial(inner_step, 0))
+    pl.semaphore_wait(barrier, n - 1 + low * (chans - 1))
+    to_all(send_first, 0)
+
+    def inner_send_step(step, slot):
+        inner_step(part, step, slot)
+
+        @pl.when(lax.rem(step, part) == part - 1)
+        def _():
+            to_all(send_first, step // part + 1)
+
+    stream(row_block - part, [lambda s, slot: load_x(part + s, slot)], inner_send_step)
     first_own().start()
+
+    for strip in range(rows // LANES):
+        span = pl.ds(strip * LANES, LANES)
+        bt_ref[span, :] = b_ref[:, span].T
 
     def back_step(step, slot):
         mg = (g_buf[slot].astype(F32) * q_buf[slot].astype(F32)).astype(BF16)
@@ -229,6 +331,12 @@
             to_all(send_second, index)
         later = [index for index in later if index not in share]
 
+    for strip in range(rows // LANES):
+        value = acc2[:, pl.ds(strip * LANES, LANES)].T
+        for b in range(LANES // row_block):
+            put_terms(1, strip * (LANES // row_block) + b, value[b * row_block:(b + 1) * row_block])
+    sum_near_start(1)
+
     second_own().wait()
     for index, (h, ch) in enumerate(chunks):
         await_second(index, recv2.at[index])
@@ -249,12 +357,33 @@
                 y_buf.at[slot, pl.ds(0, LANES)], block(dx_hbm, step), y_sem.at[slot]
             )
 
+        def term_step(step, slot):
+            acc1[...] += dot_nn(pick(0, step, cols), x_buf[slot, pl.ds(0, LANES)])
+
         def input_step(step, slot):
-            inner_grad = pick(0, step, cols)
-            y_buf[slot, pl.ds(0, LANES)] = dot_tn(inner_grad, a_ref[...]).astype(BF16)
-            acc1[...] += dot_nn(inner_grad, x_buf[slot, pl.ds(0, LANES)])
-
-        stream(PACK, [load_part], input_step, store_part)
+            y_buf[slot, pl.ds(0, LANES)] = dot_tn(pick(0, step, cols), a_ref[...]).astype(BF16)
+
+        def both_steps(step, slot):
+            input_step(step, slot)
+            term_step(step, slot)
+
+        if index < len(chunks) - 1:
+            stream(PACK, [load_part], both_steps, store_part)
+        else:
+            stream(PACK, [load_part], term_step)
+            for strip in range(n):
+                put_terms(0, strip, acc1[pl.ds(strip * row_block, row_block), :])
+            sum_near_start(0)
+            stream(PACK, [], input_step, store_part)
+        if index == 0:
+            sum_far_start(1)
+        if index == min(1, len(chunks) - 1):
+            sum_share_start(1)
+
+    sum_far_start(0)
+    sum_share_start(0)
+    sum_end(1, d2_ref)
+    sum_end(0, d1_ref)
 
     for group in range(GROUPS):
         await_first(send1.at[group])
@@ -267,6 +396,9 @@
     width, extent = inputs.shape
     cols, rows = first_factor.shape[0], second_factor.shape[0]
     row_block, col_block = rows // n, cols // n
+    chans = lax.axis_size("chan")
+    low = max(d for d in range(1, n + 1) if n % d == 0 and d * d <= n)
+    near, high, share = low * chans, n // low, row_block // chans
     chunk_count = (row_block // PACK) * (width // LANES)
     vmem = pl.BlockSpec(memory_space=pltpu.VMEM)
     hbm = pl.BlockSpec(memory_space=pl.ANY)
@@ -274,12 +406,12 @@
     long_side = max(rows, cols)
     flops = 12 * width * row_block * cols * rows
     return pl.pallas_call(
-        functools.partial(kernel, n),
+        functools.partial(kernel, n, chans, low),
         out_shape=(
             jax.ShapeDtypeStruct((width, extent), BF16),
             jax.ShapeDtypeStruct((width, extent), BF16),
-            jax.ShapeDtypeStruct((cols, cols), F32),
-            jax.ShapeDtypeStruct((rows, rows), F32),
+            jax.ShapeDtypeStruct((cols // n, cols), F32),
+            jax.ShapeDtypeStruct((rows // n, rows), F32),
         ),
         in_specs=[hbm, hbm, hbm, vmem, vmem],
         out_specs=(hbm, hbm, vmem, vmem),
@@ -293,14 +425,23 @@
             pltpu.VMEM((2, width, rows), BF16),
             pltpu.VMEM((2, width, rows), BF16),
             pltpu.VMEM((2, width, long_side), BF16),
+            pltpu.VMEM((rows, rows), BF16),
+            pltpu.VMEM((cols, cols), F32),
+            pltpu.VMEM((rows, rows), F32),
+            pltpu.VMEM((2, near, high, share, long_side), F32),
+            pltpu.VMEM((2, near, high, share, long_side), F32),
+            pltpu.VMEM((2, high, share, long_side), F32),
+            pltpu.VMEM((2, high, share, long_side), F32),
+            pltpu.VMEM((2, chans, share, long_side), F32),
             dma((2,)), dma((2,)), dma((2,)), dma((2,)), dma((2,)),
             dma((GROUPS,)), dma((GROUPS,)), dma((chunk_count,)), dma((chunk_count,)),
+            dma((3, 2)), dma((3, 2)),
         ],
         compiler_params=pltpu.CompilerParams(
-            collective_id=0, has_side_effects=True, vmem_limit_bytes=56 * 2**20
+            collective_id=0, has_side_effects=True, vmem_limit_bytes=58 * 2**20
         ),
         cost_estimate=pl.CostEstimate(flops=flops, bytes_accessed=16 * width * extent, transcendentals=0),
-    )(inputs, gate_acts, out_grad, first_factor, second_factor.T)
+    )(inputs, gate_acts, out_grad, first_factor, second_factor)
 
 
 def plain(inputs, gate_acts, out_grad, first_factor, second_factor):
@@ -337,13 +478,20 @@
     n = lax.axis_size("seq")
     width = inputs.shape[0]
     cols, rows = first_factor.shape[0], second_factor.shape[0]
-    fits = width % LANES == 0 and rows % (n * PACK) == 0 and cols % (n * PACK) == 0
+    chans = lax.axis_size("chan")
+    fits = (
+        rows == cols
+        and width % LANES == 0
+        and rows % (n * PACK) == 0
+        and LANES % (rows // n) == 0
+        and rows % (n * chans * 8) == 0
+        and chans > 1
+        and n >= 4
+    )
     args = (inputs, gate_acts, out_grad, first_factor, second_factor)
     if fits:
-        input_grad, gate_grad, first_term, second_term = fused(*args)
-        second_term = second_term.T
-    else:
-        input_grad, gate_grad, first_term, second_term = plain(*args)
+        return fused(*args)
+    input_grad, gate_grad, first_term, second_term = plain(*args)
     totals = lax.psum((first_term, second_term), "chan")
     first_grad = lax.psum_scatter(totals[0], "seq", scatter_dimension=0, tiled=True)
     second_grad = lax.psum_scatter(totals[1], "seq", scatter_dimension=0, tiled=True)

time: 570 us -> 442 us (0.78)
  waiting for transfers between devices: 159 us -> 0 us
  Pallas kernels: 370 us -> 422 us
  between operations: 13.8 us -> 0.64 us
  local copies, waits for them, and re-layouts: 23.9 us -> 16.6 us
    unnamed x4 -> x0, waiting for transfers between devices: 74 us -> none
    reduce_scatter x1 -> x0, waiting for transfers between devices: 58.8 us -> none  [local(): lax.psum_scatter(totals[0], 'seq', scatter_dimension=0, tiled=True)]
    pallas_call x1, Pallas kernels: 370 us -> 422 us  [fused(): pl.pallas_call(functools.partial(kernel, n, chans, low), out_shape=(jax.S...]
    psum x1 -> x0, waiting for transfers between devices: 26.4 us -> none  [local(): totals = lax.psum((first_term, second_term), 'chan')]
    unnamed x9 -> x8, local copies, waits for them, and re-layouts: 23.9 us -> 16.6 us
  transfers between devices with their start and end apart: 3 -> 0, of which waited for: 3 -> 0; matrix products, arithmetic and copies ran while one was open for 0% -> 0% of each run, Pallas kernels for 0% -> 0%
where the time goes in v2:
time: 442 us; the launch traced here: 439 us
  Pallas kernels  422 us (95%)
  local copies, waits for them, and re-layouts  16.6 us (4%)
    pallas_call x1, Pallas kernels, fused(): pl.pallas_call(functools.partial(kernel, n, chans, low), out_shape=(jax.S...  422 us
    unnamed x8, local copies, waits for them, and re-layouts  16.6 us

profile of v2, /device:TPU:0, one launch (start us, length us, event | category | flops | bytes accessed | tf_op | source)
XLA Modules:
  0.0 439.1 jit_solution(16345034057443120708)
XLA Ops:
  0.6 421.8 %shard_map.84 = (bf16[256,16384]{1,0:T(8,128)(2,1)}, bf16[256,16384]{1,0:T(8,128)(2,1)}, f32[32,512]{1,0:T(8,128)}, f32[32,512]{1,0:T(8,128)}) custom-call(bf16[256,16384]{1,0:T(8,128)(2,1)} %x_hbm.1, bf16[256,16384]{1,0:T(8,128)(2,1)} %q_hbm.1, bf16[256,16384]{1,0:T(8,128)(2,1)} %g_hbm.1, bf16[512,512]{1,0:T(8,128)(2,1)} %a_ref.1, bf16[512,512]{1,0:T(8,128)(2,1)} %b_ref.1), custom_call_target="tpu_custom_call" | custom-call | flops 25769803776 | bytes 67108864 | tf_op jit(solution)/shard_map/pallas_call | solution.py:408
  422.5 7.7 %copy.13 = bf16[256,16384]{1,0:T(8,128)(2,1)} copy(bf16[256,16384]{1,0:T(8,128)(2,1)} %get-tuple-element.8) | data formatting | bytes 16777216
  430.1 0.0 copy-start.1
  430.1 0.0 copy-start
  430.1 7.7 %copy.14 = bf16[256,16384]{1,0:T(8,128)(2,1)} copy(bf16[256,16384]{1,0:T(8,128)(2,1)} %get-tuple-element.9) | data formatting | bytes 16777216
  437.8 0.0 copy-done.1
  437.8 0.6 copy.15
  438.4 0.0 copy-done
  438.4 0.6 copy.16
Async XLA Ops:
  430.1 7.7 %copy-start.1 = (f32[32,512]{1,0:T(8,128)S(1)}, f32[32,512]{1,0:T(8,128)}, u32[]{:S(2)}) copy-start(f32[32,512]{1,0:T(8,128)} %get-tuple-element.10) | copy-start | bytes 196612
  430.1 8.3 %copy-start = (f32[32,512]{1,0:T(8,128)S(1)}, f32[32,512]{1,0:T(8,128)}, u32[]{:S(2)}) copy-start(f32[32,512]{1,0:T(8,128)} %get-tuple-element.11) | copy-start | bytes 196612

commit v3 on v2

--- a/solution.py
+++ b/solution.py
@@ -233,11 +233,12 @@
         )
 
     def to_all(send, index):
-        def body(d, carry):
+        def body(t, carry):
+            d = (1 - lax.rem(t, 2)) * (n // 2) + (t + 1) // 2
             send(index, hop(d)).start()
             return carry
 
-        lax.fori_loop(1, n, body, 0)
+        lax.fori_loop(0, n - 1, body, 0)
 
     def await_first(sem):
         view = got1.at[pl.ds(0, (n - 1) * part)]
@@ -360,6 +361,18 @@
         def term_step(step, slot):
             acc1[...] += dot_nn(pick(0, step, cols), x_buf[slot, pl.ds(0, LANES)])
 
+        def load_pair(which, sems):
+            return lambda step, slot: pltpu.make_async_copy(
+                block(x_hbm, 2 * step + which),
+                x_buf.at[slot, pl.ds(which * LANES, LANES)], sems.at[slot],
+            )
+
+        def pair_step(step, slot):
+            both = jnp.concatenate(
+                [pick(0, 2 * step, cols), pick(0, 2 * step + 1, cols)], axis=1
+            )
+            acc1[...] += dot_nn(both, x_buf[slot, pl.ds(0, 2 * LANES)])
+
         def input_step(step, slot):
             y_buf[slot, pl.ds(0, LANES)] = dot_tn(pick(0, step, cols), a_ref[...]).astype(BF16)
 
@@ -370,7 +383,7 @@
         if index < len(chunks) - 1:
             stream(PACK, [load_part], both_steps, store_part)
         else:
-            stream(PACK, [load_part], term_step)
+            stream(PACK // 2, [load_pair(0, x_sem), load_pair(1, g_sem)], pair_step)
             for strip in range(n):
                 put_terms(0, strip, acc1[pl.ds(strip * row_block, row_block), :])
             sum_near_start(0)
@@ -444,6 +457,25 @@
     )(inputs, gate_acts, out_grad, first_factor, second_factor)
 
 
+def copy_kernel(a_in, b_in, a_out, b_out):
+    a_out[...] = a_in[...]
+    b_out[...] = b_in[...]
+
+
+def hand_out(first, second):
+    rows = 2 * PACK
+    spec = pl.BlockSpec((rows, first.shape[1]), lambda i: (i, 0))
+    return pl.pallas_call(
+        copy_kernel,
+        out_shape=tuple(jax.ShapeDtypeStruct(v.shape, v.dtype) for v in (first, second)),
+        grid=(first.shape[0] // rows,),
+        in_specs=[spec, spec],
+        out_specs=(spec, spec),
+        compiler_params=pltpu.CompilerParams(vmem_limit_bytes=56 * 2**20),
+        cost_estimate=pl.CostEstimate(flops=0, bytes_accessed=8 * first.size, transcendentals=0),
+    )(first, second)
+
+
 def plain(inputs, gate_acts, out_grad, first_factor, second_factor):
     n = lax.axis_size("seq")
     width, extent = inputs.shape
@@ -481,7 +513,8 @@
     chans = lax.axis_size("chan")
     fits = (
         rows == cols
-        and width % LANES == 0
+        and n % 2 == 0
+        and width % (2 * LANES) == 0
         and rows % (n * PACK) == 0
         and LANES % (rows // n) == 0
         and rows % (n * chans * 8) == 0
@@ -490,7 +523,8 @@
     )
     args = (inputs, gate_acts, out_grad, first_factor, second_factor)
     if fits:
-        return fused(*args)
+        input_grad, gate_grad, first_grad, second_grad = fused(*args)
+        return *hand_out(input_grad, gate_grad), first_grad, second_grad
     input_grad, gate_grad, first_term, second_term = plain(*args)
     totals = lax.psum((first_term, second_term), "chan")
     first_grad = lax.psum_scatter(totals[0], "seq", scatter_dimension=0, tiled=True)

time: 442 us -> 429 us (0.971)
  local copies, waits for them, and re-layouts: 16.6 us -> 1.27 us
    unnamed x8 -> x6, local copies, waits for them, and re-layouts: 16.6 us -> 1.27 us
    pallas_call x0 -> x1, Pallas kernels: none -> 13.7 us  [hand_out(): pl.pallas_call(copy_kernel, out_shape=tuple((jax.ShapeDtypeStruct(v.shape...]
    pallas_call x1, Pallas kernels: 422 us -> 411 us  [fused(): pl.pallas_call(functools.partial(kernel, n, chans, low), out_shape=(jax.S...]
where the time goes in v3:
time: 429 us; the launch traced here: 427 us
  Pallas kernels  425 us (99%)
    pallas_call x1, Pallas kernels, fused(): pl.pallas_call(functools.partial(kernel, n, chans, low), out_shape=(jax.S...  411 us
    pallas_call x1, Pallas kernels, hand_out(): pl.pallas_call(copy_kernel, out_shape=tuple((jax.ShapeDtypeStruct(v.shape...  13.7 us

profile of v3, /device:TPU:0, one launch (start us, length us, event | category | flops | bytes accessed | tf_op | source)
XLA Modules:
  0.0 426.5 jit_solution(8707140356870803161)
XLA Ops:
  0.6 411.0 %shard_map.84 = (bf16[256,16384]{1,0:T(8,128)(2,1)}, bf16[256,16384]{1,0:T(8,128)(2,1)}, f32[32,512]{1,0:T(8,128)}, f32[32,512]{1,0:T(8,128)}) custom-call(bf16[256,16384]{1,0:T(8,128)(2,1)} %x_hbm.1, bf16[256,16384]{1,0:T(8,128)(2,1)} %q_hbm.1, bf16[256,16384]{1,0:T(8,128)(2,1)} %g_hbm.1, bf16[512,512]{1,0:T(8,128)(2,1)} %a_ref.1, bf16[512,512]{1,0:T(8,128)(2,1)} %b_ref.1), custom_call_target="tpu_custom_call" | custom-call | flops 25769803776 | bytes 67108864 | tf_op jit(solution)/shard_map/pallas_call | solution.py:421
  411.6 0.0 copy-start.1
  411.6 0.0 copy-start
  411.6 13.7 %shard_map.85 = (bf16[256,16384]{1,0:T(8,128)(2,1)}, bf16[256,16384]{1,0:T(8,128)(2,1)}) custom-call(bf16[256,16384]{1,0:T(8,128)(2,1)} %get-tuple-element.10.a_in, bf16[256,16384]{1,0:T(8,128)(2,1)} %get-tuple-element.11.b_in), custom_call_target="tpu_custom_call" | custom-call | bytes 33554432 | tf_op jit(solution)/shard_map/pallas_call | solution.py:468
  425.3 0.0 copy-done.1
  425.3 0.6 copy.11
  425.9 0.0 copy-done
  425.9 0.6 copy.12
Async XLA Ops:
  411.6 13.7 %copy-start.1 = (f32[32,512]{1,0:T(8,128)S(1)}, f32[32,512]{1,0:T(8,128)}, u32[]{:S(2)}) copy-start(f32[32,512]{1,0:T(8,128)} %get-tuple-element.22) | copy-start | bytes 196612
  411.6 14.3 %copy-start = (f32[32,512]{1,0:T(8,128)S(1)}, f32[32,512]{1,0:T(8,128)}, u32[]{:S(2)}) copy-start(f32[32,512]{1,0:T(8,128)} %get-tuple-element.23) | copy-start | bytes 196612

commit v4 on v3

--- a/solution.py
+++ b/solution.py
@@ -11,7 +11,6 @@
 F32 = jnp.float32
 LANES = 128
 PACK = 16
-GROUPS = 8
 
 
 def dot_nn(lhs, rhs):
@@ -24,6 +23,10 @@
 
 def dot_tn(lhs, rhs):
     return lax.dot_general(lhs, rhs, (((0,), (0,)), ((), ())), preferred_element_type=F32)
+
+
+def group_bounds(count):
+    return [0, count // 8, count // 2, count * 3 // 4, count]
 
 
 def stream(count, loads, work, store=None):
@@ -60,14 +63,15 @@
     n, chans, low, x_hbm, q_hbm, g_hbm, a_ref, b_ref,
     dx_hbm, dq_hbm, d1_ref, d2_ref,
     out1, out2, got1, got2, turned, x_buf, g_buf, q_buf, y_buf, bt_ref, acc1, acc2,
-    terms, land1, sums, land2, final,
-    x_sem, g_sem, q_sem, y_sem, own_sem, send1, recv1, send2, recv2, send_sum, recv_sum,
+    terms, land1, sums, land2, final, x_last,
+    x_sem, g_sem, q_sem, y_sem, own_sem, send1, recv1, send2, recv2, send_sum, recv_sum, last_sem,
 ):
     me, my_chan = lax.axis_index("seq"), lax.axis_index("chan")
     width = x_hbm.shape[0]
     rows, cols = b_ref.shape[0], a_ref.shape[0]
     row_block, col_block = rows // n, cols // n
-    part = row_block // GROUPS
+    bounds = group_bounds(row_block)
+    lane_parts, halves = width // LANES, row_block // PACK
 
     def hop(d):
         return lax.rem(me + d, n)
@@ -191,45 +195,36 @@
         )
 
     def send_first(group, peer):
+        first, last = bounds[group], bounds[group + 1]
         return pltpu.make_async_remote_copy(
-            src_ref=out1.at[
-                pl.ds(group * part, part), pl.ds(pl.multiple_of(peer * col_block, PACK), col_block)
-            ],
-            dst_ref=got1.at[pl.ds(me * row_block + group * part, part)],
+            src_ref=out1.at[peer, pl.ds(first, last - first)],
+            dst_ref=got1.at[pl.ds(me * row_block + first, last - first)],
             send_sem=send1.at[group], recv_sem=recv1.at[group],
             device_id={"seq": peer}, device_id_type=pl.DeviceIdType.MESH,
         )
 
     def first_own():
         return pltpu.make_async_copy(
-            out1.at[:, pl.ds(pl.multiple_of(me * col_block, PACK), col_block)],
-            got1.at[pl.ds(me * row_block, row_block)], own_sem.at[0],
-        )
-
-    def chunk_view(ref, start, count, h, ch):
-        return ref.at[
-            pl.ds(start, count), pl.ds(h * PACK, PACK), pl.ds(ch * LANES, LANES)
-        ]
-
-    lane_parts = width // LANES
-    chunks = [(h, ch) for h in range(row_block // PACK) for ch in range(lane_parts)]
+            out1.at[me], got1.at[pl.ds(me * row_block, row_block)], own_sem.at[0]
+        )
+
+    chunks = [(h, ch) for h in range(halves) for ch in range(lane_parts)]
+    sends = [(h, pl.ds(0, lane_parts)) for h in range(halves - 1)]
+    sends += [(halves - 1, pl.ds(ch, 1)) for ch in range(lane_parts)]
 
     def send_second(index, peer):
-        h, ch = chunks[index]
+        h, lanes = sends[index]
         return pltpu.make_async_remote_copy(
-            src_ref=out2.at[
-                :, pl.ds(pl.multiple_of(peer * row_block + h * PACK, PACK), PACK),
-                pl.ds(ch * LANES, LANES),
-            ],
-            dst_ref=chunk_view(got2, me * col_block, col_block, h, ch),
+            src_ref=out2.at[h, lanes, peer],
+            dst_ref=got2.at[h, lanes, pl.ds(me * col_block, col_block)],
             send_sem=send2.at[index], recv_sem=recv2.at[index],
             device_id={"seq": peer}, device_id_type=pl.DeviceIdType.MESH,
         )
 
     def second_own():
         return pltpu.make_async_copy(
-            out2.at[:, pl.ds(pl.multiple_of(me * row_block, PACK), row_block)],
-            got2.at[pl.ds(me * col_block, col_block)], own_sem.at[1],
+            out2.at[:, :, me],
+            got2.at[:, :, pl.ds(me * col_block, col_block)], own_sem.at[1],
         )
 
     def to_all(send, index):
@@ -240,30 +235,24 @@
 
         lax.fori_loop(0, n - 1, body, 0)
 
-    def await_first(sem):
-        view = got1.at[pl.ds(0, (n - 1) * part)]
-        pltpu.make_async_copy(view, view, sem).wait()
-
-    def await_second(index, sem):
-        h, ch = chunks[index]
-        view = chunk_view(got2, 0, (n - 1) * col_block, h, ch)
-        pltpu.make_async_copy(view, view, sem).wait()
-
-    def inner_step(first, step, slot):
-        out1[first + step] = dot_nt(a_ref[...], x_buf[slot]).astype(BF16)
-
-    stream(part, [load_x], functools.partial(inner_step, 0))
-    pl.semaphore_wait(barrier, n - 1 + low * (chans - 1))
-    to_all(send_first, 0)
-
-    def inner_send_step(step, slot):
-        inner_step(part, step, slot)
-
-        @pl.when(lax.rem(step, part) == part - 1)
-        def _():
-            to_all(send_first, step // part + 1)
-
-    stream(row_block - part, [lambda s, slot: load_x(part + s, slot)], inner_send_step)
+    def await_first(group, sems):
+        view = got1.at[pl.ds(0, (n - 1) * (bounds[group + 1] - bounds[group]))]
+        pltpu.make_async_copy(view, view, sems.at[group]).wait()
+
+    def await_second(index, sems):
+        h, lanes = sends[index]
+        view = got2.at[h, lanes, pl.ds(0, (n - 1) * col_block)]
+        pltpu.make_async_copy(view, view, sems.at[index]).wait()
+
+    for group, first in enumerate(bounds[:-1]):
+        def inner_step(step, slot):
+            value = dot_nt(a_ref[...], x_buf[slot]).astype(BF16)
+            out1[:, first + step] = value.reshape(n, col_block, width)
+
+        stream(bounds[group + 1] - first, [lambda s, slot: load_x(first + s, slot)], inner_step)
+        if group == 0:
+            pl.semaphore_wait(barrier, n - 1 + low * (chans - 1))
+        to_all(send_first, group)
     first_own().start()
 
     for strip in range(rows // LANES):
@@ -272,7 +261,9 @@
 
     def back_step(step, slot):
         mg = (g_buf[slot].astype(F32) * q_buf[slot].astype(F32)).astype(BF16)
-        out2[step] = dot_nt(bt_ref[...], mg).astype(BF16)
+        value = dot_nt(bt_ref[...], mg).astype(BF16).reshape(n, halves, PACK, width)
+        for h, ch in chunks:
+            out2[h, ch, :, step] = value[:, h, :, ch * LANES:(ch + 1) * LANES]
 
     stream(col_block, [load_g, load_q], back_step)
     second_own().start()
@@ -280,18 +271,18 @@
     acc1[...] = jnp.zeros_like(acc1)
     acc2[...] = jnp.zeros_like(acc2)
 
-    for group in range(GROUPS - 1):
-        await_first(recv1.at[group])
-    early = max(len(chunks) // 2, 1)
-    for index in range(early):
-        to_all(send_second, index)
-    await_first(recv1.at[GROUPS - 1])
+    groups = len(bounds) - 1
+    for group in range(groups - 1):
+        await_first(group, recv1)
+    to_all(send_second, 0)
+    await_first(groups - 1, recv1)
+    if len(sends) > 1:
+        to_all(send_second, 1)
     first_own().wait()
 
-    def turn(got, h, ch, slot, total):
+    def turn(got, slot, total):
         def body(block, carry):
-            start = pl.multiple_of(block * 8, 8)
-            value = got[pl.ds(start, 8), pl.ds(h * PACK, PACK), pl.ds(ch * LANES, LANES)]
+            value = got(pl.ds(pl.multiple_of(block * 8, 8), 8))
             turned[slot, pl.ds(pl.multiple_of(block * 8 * PACK, 8 * PACK), 8 * PACK), :] = (
                 value.astype(F32).reshape(8 * PACK, LANES)
             )
@@ -302,11 +293,10 @@
     def pick(slot, step, total):
         return turned[slot, pl.ds(step, total, stride=PACK), :].astype(BF16)
 
-    later = list(range(early, len(chunks)))
-    halves = col_block // PACK
-    for h in range(halves):
+    for h in range(col_block // PACK):
         for ch in range(lane_parts):
-            turn(got1, h, ch, ch, rows)
+            lanes = pl.ds(ch * LANES, LANES)
+            turn(lambda span: got1[span, pl.ds(h * PACK, PACK), lanes], ch, rows)
 
         def gate_step(step, slot):
             g = g_buf[slot].astype(F32)
@@ -327,10 +317,9 @@
             [lambda s, slot: load_g(h * PACK + s, slot), lambda s, slot: load_q(h * PACK + s, slot)],
             gate_step, store_dq,
         )
-        share = later if h == halves - 1 else later[: max(len(later) // 2, 0)]
-        for index in share:
-            to_all(send_second, index)
-        later = [index for index in later if index not in share]
+        if h == 0:
+            for index in range(2, len(sends)):
+                to_all(send_second, index)
 
     for strip in range(rows // LANES):
         value = acc2[:, pl.ds(strip * LANES, LANES)].T
@@ -338,10 +327,23 @@
             put_terms(1, strip * (LANES // row_block) + b, value[b * row_block:(b + 1) * row_block])
     sum_near_start(1)
 
+    def last_x(index, step):
+        h, ch = chunks[index]
+        start = (h * PACK + step) * cols
+        return pltpu.make_async_copy(
+            x_hbm.at[pl.ds(ch * LANES, LANES), pl.ds(start, cols)],
+            x_last.at[step // 2, pl.ds(step % 2 * LANES, LANES)], last_sem.at[step],
+        )
+
     second_own().wait()
     for index, (h, ch) in enumerate(chunks):
-        await_second(index, recv2.at[index])
-        turn(got2, h, ch, 0, cols)
+        last = index == len(chunks) - 1
+        if last:
+            for step in range(PACK):
+                last_x(index, step).start()
+        if h == halves - 1 or ch == 0:
+            await_second(h if h < halves - 1 else h + ch, recv2)
+        turn(lambda span: got2[h, ch, span], 0, cols)
         span = pl.ds(ch * LANES, LANES)
 
         def block(ref, step):
@@ -361,17 +363,12 @@
         def term_step(step, slot):
             acc1[...] += dot_nn(pick(0, step, cols), x_buf[slot, pl.ds(0, LANES)])
 
-        def load_pair(which, sems):
-            return lambda step, slot: pltpu.make_async_copy(
-                block(x_hbm, 2 * step + which),
-                x_buf.at[slot, pl.ds(which * LANES, LANES)], sems.at[slot],
-            )
-
-        def pair_step(step, slot):
+        def pair_step(step, carry):
             both = jnp.concatenate(
                 [pick(0, 2 * step, cols), pick(0, 2 * step + 1, cols)], axis=1
             )
-            acc1[...] += dot_nn(both, x_buf[slot, pl.ds(0, 2 * LANES)])
+            acc1[...] += dot_nn(both, x_last[step])
+            return carry
 
         def input_step(step, slot):
             y_buf[slot, pl.ds(0, LANES)] = dot_tn(pick(0, step, cols), a_ref[...]).astype(BF16)
@@ -380,10 +377,12 @@
             input_step(step, slot)
             term_step(step, slot)
 
-        if index < len(chunks) - 1:
+        if not last:
             stream(PACK, [load_part], both_steps, store_part)
         else:
-            stream(PACK // 2, [load_pair(0, x_sem), load_pair(1, g_sem)], pair_step)
+            for step in range(PACK):
+                last_x(index, step).wait()
+            lax.fori_loop(0, PACK // 2, pair_step, 0)
             for strip in range(n):
                 put_terms(0, strip, acc1[pl.ds(strip * row_block, row_block), :])
             sum_near_start(0)
@@ -398,10 +397,10 @@
     sum_end(1, d2_ref)
     sum_end(0, d1_ref)
 
-    for group in range(GROUPS):
-        await_first(send1.at[group])
-    for index in range(len(chunks)):
-        await_second(index, send2.at[index])
+    for group in range(groups):
+        await_first(group, send1)
+    for index in range(len(sends)):
+        await_second(index, send2)
 
 
 def fused(inputs, gate_acts, out_grad, first_factor, second_factor):
@@ -412,7 +411,8 @@
     chans = lax.axis_size("chan")
     low = max(d for d in range(1, n + 1) if n % d == 0 and d * d <= n)
     near, high, share = low * chans, n // low, row_block // chans
-    chunk_count = (row_block // PACK) * (width // LANES)
+    halves, lane_parts = row_block // PACK, width // LANES
+    groups, chunk_count = len(group_bounds(row_block)) - 1, halves - 1 + lane_parts
     vmem = pl.BlockSpec(memory_space=pltpu.VMEM)
     hbm = pl.BlockSpec(memory_space=pl.ANY)
     dma = pltpu.SemaphoreType.DMA
@@ -429,10 +429,10 @@
         in_specs=[hbm, hbm, hbm, vmem, vmem],
         out_specs=(hbm, hbm, vmem, vmem),
         scratch_shapes=[
-            pltpu.VMEM((row_block, cols, width), BF16),
-            pltpu.VMEM((col_block, rows, width), BF16),
+            pltpu.VMEM((n, row_block, col_block, width), BF16),
+            pltpu.VMEM((halves, lane_parts, n, col_block, PACK, LANES), BF16),
             pltpu.VMEM((rows, col_block, width), BF16),
-            pltpu.VMEM((cols, row_block, width), BF16),
+            pltpu.VMEM((halves, lane_parts, cols, PACK, LANES), BF16),
             pltpu.VMEM((width // LANES, long_side * PACK, LANES), F32),
             pltpu.VMEM((2, width, cols), BF16),
             pltpu.VMEM((2, width, rows), BF16),
@@ -446,9 +446,10 @@
             pltpu.VMEM((2, high, share, long_side), F32),
             pltpu.VMEM((2, high, share, long_side), F32),
             pltpu.VMEM((2, chans, share, long_side), F32),
+            pltpu.VMEM((PACK // 2, 2 * LANES, cols), BF16),
             dma((2,)), dma((2,)), dma((2,)), dma((2,)), dma((2,)),
-            dma((GROUPS,)), dma((GROUPS,)), dma((chunk_count,)), dma((chunk_count,)),
-            dma((3, 2)), dma((3, 2)),
+            dma((groups,)), dma((groups,)), dma((chunk_count,)), dma((chunk_count,)),
+            dma((3, 2)), dma((3, 2)), dma((PACK,)),
         ],
         compiler_params=pltpu.CompilerParams(
             collective_id=0, has_side_effects=True, vmem_limit_bytes=58 * 2**20

time: 429 us -> 428 us (level)
  no operation moved by 1% of the time
where the time goes in v4:
time: 428 us; the launch traced here: 425 us
  Pallas kernels  423 us (99%)
    pallas_call x1, Pallas kernels, fused(): pl.pallas_call(functools.partial(kernel, n, chans, low), out_shape=(jax.S...  409 us
    pallas_call x1, Pallas kernels, hand_out(): pl.pallas_call(copy_kernel, out_shape=tuple((jax.ShapeDtypeStruct(v.shape...  13.7 us

profile of v4, /device:TPU:0, one launch (start us, length us, event | category | flops | bytes accessed | tf_op | source)
XLA Modules:
  0.0 424.9 jit_solution(13988643526602314583)
XLA Ops:
  0.6 409.3 %shard_map.84 = (bf16[256,16384]{1,0:T(8,128)(2,1)}, bf16[256,16384]{1,0:T(8,128)(2,1)}, f32[32,512]{1,0:T(8,128)}, f32[32,512]{1,0:T(8,128)}) custom-call(bf16[256,16384]{1,0:T(8,128)(2,1)} %x_hbm.1, bf16[256,16384]{1,0:T(8,128)(2,1)} %q_hbm.1, bf16[256,16384]{1,0:T(8,128)(2,1)} %g_hbm.1, bf16[512,512]{1,0:T(8,128)(2,1)} %a_ref.1, bf16[512,512]{1,0:T(8,128)(2,1)} %b_ref.1), custom_call_target="tpu_custom_call" | custom-call | flops 25769803776 | bytes 67108864 | tf_op jit(solution)/shard_map/pallas_call | solution.py:421
  410.0 0.0 copy-start.1
  410.0 0.0 copy-start
  410.0 13.7 %shard_map.85 = (bf16[256,16384]{1,0:T(8,128)(2,1)}, bf16[256,16384]{1,0:T(8,128)(2,1)}) custom-call(bf16[256,16384]{1,0:T(8,128)(2,1)} %get-tuple-element.10.a_in, bf16[256,16384]{1,0:T(8,128)(2,1)} %get-tuple-element.11.b_in), custom_call_target="tpu_custom_call" | custom-call | bytes 33554432 | tf_op jit(solution)/shard_map/pallas_call | solution.py:469
  423.6 0.0 copy-done.1
  423.6 0.6 copy.11
  424.3 0.0 copy-done
  424.3 0.6 copy.12
Async XLA Ops:
  410.0 13.7 %copy-start.1 = (f32[32,512]{1,0:T(8,128)S(1)}, f32[32,512]{1,0:T(8,128)}, u32[]{:S(2)}) copy-start(f32[32,512]{1,0:T(8,128)} %get-tuple-element.22) | copy-start | bytes 196612
  410.0 14.3 %copy-start = (f32[32,512]{1,0:T(8,128)S(1)}, f32[32,512]{1,0:T(8,128)}, u32[]{:S(2)}) copy-start(f32[32,512]{1,0:T(8,128)} %get-tuple-element.23) | copy-start | bytes 196612

commit v5 on v4

--- a/solution.py
+++ b/solution.py
@@ -63,7 +63,7 @@
     n, chans, low, x_hbm, q_hbm, g_hbm, a_ref, b_ref,
     dx_hbm, dq_hbm, d1_ref, d2_ref,
     out1, out2, got1, got2, turned, x_buf, g_buf, q_buf, y_buf, bt_ref, acc1, acc2,
-    terms, land1, sums, land2, final, x_last,
+    terms, land1, sums, land2, whole, x_last,
     x_sem, g_sem, q_sem, y_sem, own_sem, send1, recv1, send2, recv2, send_sum, recv_sum, last_sem,
 ):
     me, my_chan = lax.axis_index("seq"), lax.axis_index("chan")
@@ -95,11 +95,12 @@
         pltpu.make_async_copy(view, view, recv_sum.at[kind, which]).wait()
         pltpu.make_async_copy(view, view, send_sum.at[kind, which]).wait()
 
-    def sum_near_start(which):
+    def sum_near_start(which, first, count):
         def body(d, carry):
             slot, device = near_device(d)
+            span = pl.ds(first, count)
             remote(
-                terms.at[which, slot], land1.at[which, my_near], 0, which, device
+                terms.at[which, slot, span], land1.at[which, my_near, span], 0, which, device
             ).start()
             return carry
 
@@ -115,38 +116,28 @@
 
         lax.fori_loop(1, near, add, 0)
 
+        land2[which, my_chan, my_high] = sums[which, my_high]
+
         def body(d, carry):
-            to = lax.rem(my_high + d, high)
+            spot = lax.rem(my_high * chans + my_chan + d, high * chans)
+            to = spot // chans
             remote(
-                sums.at[which, to], land2.at[which, my_high], 1, which,
-                {"seq": to * low + my_low, "chan": my_chan},
+                sums.at[which, to], land2.at[which, my_chan, my_high], 1, which,
+                {"seq": to * low + my_low, "chan": lax.rem(spot, chans)},
             ).start()
             return carry
 
-        lax.fori_loop(1, high, body, 0)
-
-    def sum_share_start(which):
-        await_sum(land2.at[which, pl.ds(0, high - 1)], 1, which)
-        final[which, my_chan] = sums[which, my_high]
-
-        def add(d, carry):
-            final[which, my_chan] += land2[which, lax.rem(my_high + d, high)]
-            return carry
-
-        lax.fori_loop(1, high, add, 0)
-
-        def body(d, carry):
-            remote(
-                final.at[which, my_chan], final.at[which, my_chan], 2, which,
-                {"seq": me, "chan": lax.rem(my_chan + d, chans)},
-            ).start()
-            return carry
-
-        lax.fori_loop(1, chans, body, 0)
+        lax.fori_loop(1, high * chans, body, 0)
 
     def sum_end(which, out):
-        await_sum(final.at[which, pl.ds(0, chans - 1)], 2, which)
-        out[...] = final[which].reshape(out.shape)
+        share = row_block // chans
+        view = whole.at[pl.ds(0, high * chans - 1)]
+        await_sum(view, 1, which)
+        for c in range(chans):
+            total = land2[which, c, 0]
+            for part in range(1, high):
+                total += land2[which, c, part]
+            out[pl.ds(c * share, share), :] = total
 
     def put_terms(which, strip, value):
         share = row_block // chans
@@ -156,25 +147,15 @@
     barrier = pltpu.get_barrier_semaphore()
 
     def greet(d, carry):
+        spot = lax.rem(me * chans + my_chan + d, n * chans)
         pl.semaphore_signal(
-            barrier, inc=1, device_id={"seq": hop(d)}, device_id_type=pl.DeviceIdType.MESH
+            barrier, inc=1,
+            device_id={"seq": spot // chans, "chan": lax.rem(spot, chans)},
+            device_id_type=pl.DeviceIdType.MESH,
         )
         return carry
 
-    lax.fori_loop(1, n, greet, 0)
-
-    def greet_chan(d, carry):
-        def body(spot, inner):
-            pl.semaphore_signal(
-                barrier, inc=1,
-                device_id={"seq": my_high * low + spot, "chan": lax.rem(my_chan + d, chans)},
-                device_id_type=pl.DeviceIdType.MESH,
-            )
-            return inner
-
-        return lax.fori_loop(0, low, body, carry)
-
-    lax.fori_loop(1, chans, greet_chan, 0)
+    lax.fori_loop(1, n * chans, greet, 0)
 
     def load_x(step, slot):
         return pltpu.make_async_copy(
@@ -251,7 +232,7 @@
 
         stream(bounds[group + 1] - first, [lambda s, slot: load_x(first + s, slot)], inner_step)
         if group == 0:
-            pl.semaphore_wait(barrier, n - 1 + low * (chans - 1))
+            pl.semaphore_wait(barrier, n * chans - 1)
         to_all(send_first, group)
     first_own().start()
 
@@ -325,7 +306,7 @@
         value = acc2[:, pl.ds(strip * LANES, LANES)].T
         for b in range(LANES // row_block):
             put_terms(1, strip * (LANES // row_block) + b, value[b * row_block:(b + 1) * row_block])
-    sum_near_start(1)
+    sum_near_start(1, 0, high)
 
     def last_x(index, step):
         h, ch = chunks[index]
@@ -363,13 +344,6 @@
         def term_step(step, slot):
             acc1[...] += dot_nn(pick(0, step, cols), x_buf[slot, pl.ds(0, LANES)])
 
-        def pair_step(step, carry):
-            both = jnp.concatenate(
-                [pick(0, 2 * step, cols), pick(0, 2 * step + 1, cols)], axis=1
-            )
-            acc1[...] += dot_nn(both, x_last[step])
-            return carry
-
         def input_step(step, slot):
             y_buf[slot, pl.ds(0, LANES)] = dot_tn(pick(0, step, cols), a_ref[...]).astype(BF16)
 
@@ -382,18 +356,34 @@
         else:
             for step in range(PACK):
                 last_x(index, step).wait()
-            lax.fori_loop(0, PACK // 2, pair_step, 0)
-            for strip in range(n):
-                put_terms(0, strip, acc1[pl.ds(strip * row_block, row_block), :])
-            sum_near_start(0)
+            strips = 2 if high % 2 == 0 else 1
+            tall = cols // strips
+            for strip in range(strips):
+                span_rows = pl.ds(strip * tall, tall)
+
+                def pair_step(step, carry):
+                    both = jnp.concatenate(
+                        [
+                            turned[
+                                0, pl.ds(strip * tall * PACK + 2 * step + odd, tall, stride=PACK), :
+                            ].astype(BF16)
+                            for odd in range(2)
+                        ],
+                        axis=1,
+                    )
+                    acc1[span_rows, :] += dot_nn(both, x_last[step])
+                    return carry
+
+                lax.fori_loop(0, PACK // 2, pair_step, 0)
+                owners = n // strips
+                for owner in range(strip * owners, (strip + 1) * owners):
+                    put_terms(0, owner, acc1[pl.ds(owner * row_block, row_block), :])
+                sum_near_start(0, strip * (high // strips), high // strips)
             stream(PACK, [], input_step, store_part)
         if index == 0:
             sum_far_start(1)
-        if index == min(1, len(chunks) - 1):
-            sum_share_start(1)
 
     sum_far_start(0)
-    sum_share_start(0)
     sum_end(1, d2_ref)
     sum_end(0, d1_ref)
 
@@ -444,8 +434,8 @@
             pltpu.VMEM((2, near, high, share, long_side), F32),
             pltpu.VMEM((2, near, high, share, long_side), F32),
             pltpu.VMEM((2, high, share, long_side), F32),
-            pltpu.VMEM((2, high, share, long_side), F32),
-            pltpu.VMEM((2, chans, share, long_side), F32),
+            pltpu.VMEM((2, chans, high, share, long_side), F32),
+            pltpu.VMEM((high * chans, share, long_side), F32),
             pltpu.VMEM((PACK // 2, 2 * LANES, cols), BF16),
             dma((2,)), dma((2,)), dma((2,)), dma((2,)), dma((2,)),
             dma((groups,)), dma((groups,)), dma((chunk_count,)), dma((chunk_count,)),
@@ -458,20 +448,41 @@
     )(inputs, gate_acts, out_grad, first_factor, second_factor)
 
 
-def copy_kernel(a_in, b_in, a_out, b_out):
-    a_out[...] = a_in[...]
-    b_out[...] = b_in[...]
+def copy_kernel(a_in, b_in, a_out, b_out, held, in_sem, out_sem):
+    pieces, rows = held.shape[1], held.shape[2]
+
+    def move(which, piece, inward):
+        span = pl.ds(piece * rows, rows)
+        if inward:
+            source = (a_in, b_in)[which].at[span]
+            return pltpu.make_async_copy(source, held.at[which, piece], in_sem.at[which, piece])
+        target = (a_out, b_out)[which].at[span]
+        return pltpu.make_async_copy(held.at[which, piece], target, out_sem.at[which, piece])
+
+    order = [(which, piece) for piece in range(pieces) for which in range(2)]
+    for spot in order:
+        move(*spot, True).start()
+    for spot in order:
+        move(*spot, True).wait()
+        move(*spot, False).start()
+    for spot in order:
+        move(*spot, False).wait()
 
 
 def hand_out(first, second):
     rows = 2 * PACK
-    spec = pl.BlockSpec((rows, first.shape[1]), lambda i: (i, 0))
+    pieces = first.shape[0] // rows
+    hbm = pl.BlockSpec(memory_space=pl.ANY)
+    dma = pltpu.SemaphoreType.DMA
     return pl.pallas_call(
         copy_kernel,
         out_shape=tuple(jax.ShapeDtypeStruct(v.shape, v.dtype) for v in (first, second)),
-        grid=(first.shape[0] // rows,),
-        in_specs=[spec, spec],
-        out_specs=(spec, spec),
+        in_specs=[hbm, hbm],
+        out_specs=(hbm, hbm),
+        scratch_shapes=[
+            pltpu.VMEM((2, pieces, rows, first.shape[1]), first.dtype),
+            dma((2, pieces)), dma((2, pieces)),
+        ],
         compiler_params=pltpu.CompilerParams(vmem_limit_bytes=56 * 2**20),
         cost_estimate=pl.CostEstimate(flops=0, bytes_accessed=8 * first.size, transcendentals=0),
     )(first, second)

time: 428 us -> 410 us (0.958)
  Pallas kernels: 423 us -> 406 us
    pallas_call x1, Pallas kernels: 409 us -> 394 us  [fused(): pl.pallas_call(functools.partial(kernel, n, chans, low), out_shape=(jax.S...]
where the time goes in v5:
time: 410 us; the launch traced here: 408 us
  Pallas kernels  406 us (99%)
    pallas_call x1, Pallas kernels, fused(): pl.pallas_call(functools.partial(kernel, n, chans, low), out_shape=(jax.S...  394 us
    pallas_call x1, Pallas kernels, hand_out(): pl.pallas_call(copy_kernel, out_shape=tuple((jax.ShapeDtypeStruct(v.shape...  12 us

profile of v5, /device:TPU:0, one launch (start us, length us, event | category | flops | bytes accessed | tf_op | source)
XLA Modules:
  0.0 407.7 jit_solution(13880839383394011180)
XLA Ops:
  0.6 393.8 %shard_map.84 = (bf16[256,16384]{1,0:T(8,128)(2,1)}, bf16[256,16384]{1,0:T(8,128)(2,1)}, f32[32,512]{1,0:T(8,128)}, f32[32,512]{1,0:T(8,128)}) custom-call(bf16[256,16384]{1,0:T(8,128)(2,1)} %x_hbm.1, bf16[256,16384]{1,0:T(8,128)(2,1)} %q_hbm.1, bf16[256,16384]{1,0:T(8,128)(2,1)} %g_hbm.1, bf16[512,512]{1,0:T(8,128)(2,1)} %a_ref.1, bf16[512,512]{1,0:T(8,128)(2,1)} %b_ref.1), custom_call_target="tpu_custom_call" | custom-call | flops 25769803776 | bytes 67108864 | tf_op jit(solution)/shard_map/pallas_call | solution.py:411
  394.4 0.0 copy-start.1
  394.4 0.0 copy-start
  394.5 12.0 %shard_map.85 = (bf16[256,16384]{1,0:T(8,128)(2,1)}, bf16[256,16384]{1,0:T(8,128)(2,1)}) custom-call(bf16[256,16384]{1,0:T(8,128)(2,1)} %get-tuple-element.10.a_in, bf16[256,16384]{1,0:T(8,128)(2,1)} %get-tuple-element.11.b_in), custom_call_target="tpu_custom_call" | custom-call | bytes 33554432 | tf_op jit(solution)/shard_map/pallas_call | solution.py:477
  406.5 0.0 copy-done.1
  406.5 0.6 copy.11
  407.1 0.0 copy-done
  407.1 0.6 copy.12
Async XLA Ops:
  394.4 12.0 %copy-start.1 = (f32[32,512]{1,0:T(8,128)S(1)}, f32[32,512]{1,0:T(8,128)}, u32[]{:S(2)}) copy-start(f32[32,512]{1,0:T(8,128)} %get-tuple-element.22) | copy-start | bytes 196612
  394.4 12.7 %copy-start = (f32[32,512]{1,0:T(8,128)S(1)}, f32[32,512]{1,0:T(8,128)}, u32[]{:S(2)}) copy-start(f32[32,512]{1,0:T(8,128)} %get-tuple-element.23) | copy-start | bytes 196612
